TPU v7x, 32 devices: a whole 2x2x4 slice. The times are simulated.
32 devices in a mesh: groups: 2 (over y), tile: 4 (over z), plane: 2 (over x), inst: 2 (over core).
Axes of the slice: x: 2, y: 2, z: 4, core: 2. Of those that a mesh axis runs over, the one named last changes fastest.
Arguments:
- state: float32 [48, 10, 2, 32, 128], P('inst', 'groups', 'plane', 'tile'), parts along dimension 1, may hold values from -6 to 6
- boundary: float32 [48, 2, 10, 32, 128], P('inst', None, 'groups', ('tile', 'plane')), parts along dimension 2, may hold values from -6 to 6
- inv_volume: float32 [4, 32, 128], P(('groups', 'plane'), 'tile'), parts along dimension 0, may hold values from 0.5 to 2
- flux_matrix: float32 [6, 5, 5], P('groups'), parts along dimension 0, may hold values from -2.5 to 2.5
- left_vectors: float32 [10, 5], P('groups'), parts along dimension 0, may hold values from -2.5 to 2.5
- right_vectors: float32 [10, 5], P('groups'), parts along dimension 0, may hold values from -2.5 to 2.5
- gain: float32 [4, 2, 64, 2, 3], P('groups'), parts along dimension 0, may hold values from -3 to 3
- harmonic_index: int32 [40], P('groups'), parts along dimension 0, may hold values from 1 to 23, as said below
- mode_count: int32 [4, 128], P('groups'), parts along dimension 0, may hold values from 1 to 64
Outputs:
- residual: float32 [48, 10, 2, 32, 128], P('inst', 'groups', 'plane', 'tile'), parts along dimension 1
- corrected: float32 [48, 2, 10, 32, 128], P('inst', None, 'groups', ('tile', 'plane')), parts along dimension 2
There are 2 independent parts, one for each index of `groups`. A program takes and returns all parts, laid end to end along the dimension named above; each array names one. Nothing has to cross between parts.
Inputs may be any that keep to these rules, and one draw needn't show every extreme that they name: `harmonic_index`: 20 distinct values in rising order; the first is 1 and the last is 23.
All inputs are finite; a program needn't handle non-finite values.
Results may differ from a plain program's by a relative error of at most 0.0001.
Values sent between devices are 32-bit elements; how exact they have to be, the bound alone decides.
A program may use at most 64 MiB of HBM per device.

v0:
```python
import functools
import math

import jax
import jax.numpy as jnp
import numpy as np
from jax import lax
from jax.experimental import pallas as pl
from jax.experimental.pallas import tpu as pltpu
from jax.sharding import PartitionSpec as P

NI = 2


precise = lax.Precision.HIGHEST
DISSIPATION = 0.25
OMEGA_SCALE = 0.1


def padded_2(x, sides, width):
    for axis, dim in sides:
        size, length = (lax.axis_size(axis), x.shape[dim])
        up = [(i, (i + 1) % size) for i in range(size)]
        down = [(j, i) for i, j in up]
        last = lax.slice_in_dim(x, length - width, length, axis=dim)
        initial = lax.slice_in_dim(x, 0, width, axis=dim)
        before = lax.ppermute(last, axis, up)
        after = lax.ppermute(initial, axis, down)
        x = jnp.concatenate([before, x, after], axis=dim)
    return x


def cell_tables(cell_ids, mode_total, period):
    product = cell_ids[:, None] * jnp.arange(mode_total, dtype=jnp.int32)[None, :] % period
    phases = product.astype(jnp.float32) * (2.0 * math.pi / period)
    return (jnp.cos(phases), jnp.sin(phases))


def time_tables(harmonic_index, instance_ids, period):
    product = instance_ids[:, None] * harmonic_index[None, :] % period
    phases = product.astype(jnp.float32) * (2.0 * math.pi / period)
    cos_table = jnp.cos(phases)
    sin_table = jnp.sin(phases)
    frequency = harmonic_index.astype(jnp.float32)[None, :]
    analysis = jnp.concatenate([cos_table, sin_table], axis=1).T * (2.0 / period)
    synthesis = (
        jnp.concatenate([-frequency * sin_table, frequency * cos_table], axis=1) * OMEGA_SCALE
    )
    return (analysis, synthesis)


def correct_block(block, cell_ids, period, left_vectors, right_vectors, gain, resolved):
    mode_total = gain.shape[2]
    cos_table, sin_table = cell_tables(cell_ids, mode_total, period)
    both_tables = jnp.concatenate([cos_table, sin_table], axis=1)
    spectrum = jnp.einsum("tpvcr,cm->tpvmr", block, both_tables * (2.0 / period), precision=precise)
    hat_cos = spectrum[:, :, :, :mode_total]
    hat_sin = spectrum[:, :, :, mode_total:]
    wave_cos = jnp.einsum("uv,tpvmr->tpumr", left_vectors, hat_cos, precision=precise)
    wave_sin = jnp.einsum("uv,tpvmr->tpumr", left_vectors, hat_sin, precision=precise)
    gain_real = gain[:, 0]
    gain_imag = gain[:, 1]
    out_cos = wave_cos[:, :, NI:]
    out_sin = wave_sin[:, :, NI:]
    target_cos = jnp.einsum(
        "pmio,tpomr->tpimr", gain_real, out_cos, precision=precise
    ) - jnp.einsum("pmio,tpomr->tpimr", gain_imag, out_sin, precision=precise)
    target_sin = jnp.einsum(
        "pmio,tpomr->tpimr", gain_imag, out_cos, precision=precise
    ) + jnp.einsum("pmio,tpomr->tpimr", gain_real, out_sin, precision=precise)
    jump_cos = (target_cos - wave_cos[:, :, :NI]) * resolved[None, :, None]
    jump_sin = (target_sin - wave_sin[:, :, :NI]) * resolved[None, :, None]
    back_cos = jnp.einsum("ui,tpimr->tpumr", right_vectors[:, :NI], jump_cos, precision=precise)
    back_sin = jnp.einsum("ui,tpimr->tpumr", right_vectors[:, :NI], jump_sin, precision=precise)
    joined = jnp.concatenate([back_cos, back_sin], axis=3)
    delta = jnp.einsum("tpumr,cm->tpucr", joined, both_tables, precision=precise)
    return block + delta


def local(
    state,
    boundary,
    inv_volume,
    flux_matrix,
    left_vectors,
    right_vectors,
    gain,
    harmonic_index,
    mode_count,
):
    tiles = lax.axis_size("tile")
    planes = lax.axis_size("plane")
    face_cells = boundary.shape[3]
    period = face_cells * tiles * planes
    local_stations = boundary.shape[4] // (tiles * planes)
    station = lax.axis_index("tile") * planes + lax.axis_index("plane")
    station_modes = lax.dynamic_slice_in_dim(
        mode_count, station * local_stations, local_stations, 1
    )
    resolved = (
        jnp.arange(gain.shape[2], dtype=jnp.int32)[None, :, None] < station_modes[:, None, :]
    ).astype(jnp.float32)
    natural_ids = jnp.arange(period, dtype=jnp.int32)
    fixed = correct_block(
        lax.all_to_all(boundary, ("tile", "plane"), split_axis=4, concat_axis=3, tiled=True),
        natural_ids,
        period,
        left_vectors,
        right_vectors,
        gain,
        resolved,
    )
    corrected = lax.all_to_all(fixed, ("tile", "plane"), split_axis=3, concat_axis=4, tiled=True)
    padded = padded_2(state, (("tile", 3), ("plane", 2)), 1)
    layers = lax.all_gather(corrected, "plane", axis=3, tiled=True)
    plane_pos = lax.axis_index("plane")
    centre = padded[:, :, :, 1:-1]
    inlet_layer = jnp.where(plane_pos == 0, layers[:, 0], centre[:, :, 0])
    exit_layer = jnp.where(plane_pos == planes - 1, layers[:, 1], centre[:, :, -1])
    axial = jnp.concatenate([inlet_layer[:, :, None], state, exit_layer[:, :, None]], axis=2)
    radial = jnp.pad(state, ((0, 0), (0, 0), (0, 0), (0, 0), (1, 1)))
    middle = padded[:, :, 1:-1]
    neighbours = (
        (axial[:, :, 2:], axial[:, :, :-2]),
        (middle[:, :, :, 2:], middle[:, :, :, :-2]),
        (radial[..., 2:], radial[..., :-2]),
    )
    total = jnp.zeros_like(state)
    for direction in range(3):
        forward, backward = neighbours[direction]
        total = total + jnp.einsum(
            "vw,twacr->tvacr", flux_matrix[direction], 0.5 * (forward - backward), precision=precise
        )
        total = total - DISSIPATION * (forward - 2.0 * state + backward)
    flux = inv_volume[None, None] * total
    local_count = state.shape[0]
    total_count = local_count * lax.axis_size("inst")
    instance_ids = lax.axis_index("inst") * local_count + jnp.arange(local_count, dtype=jnp.int32)
    analysis_local, synthesis_local = time_tables(harmonic_index, instance_ids, total_count)
    flat_state = state.reshape(local_count, -1)
    analysis_full, unused_table = time_tables(
        harmonic_index, jnp.arange(total_count, dtype=jnp.int32), total_count
    )
    combined = jnp.dot(synthesis_local, analysis_full, precision=precise)
    rate = jnp.dot(
        combined, lax.all_gather(flat_state, "inst", axis=0, tiled=True), precision=precise
    )
    residual = flux + rate.reshape(state.shape)
    return (residual, corrected)


def fast_kernel(
    sizes,
    state,
    boundary,
    volume,
    flux_m,
    left_m,
    right_m,
    columns,
    counts,
    taps,
    analysis,
    synthesis,
    residual,
    corrected,
    own,
    twin,
    beside,
    faces,
    halves,
    spread,
    out8,
    out4,
    in8,
    in4,
    edges,
    below,
    above,
    taps_wide,
    gains,
    resolved,
    local_sem,
    swap_send,
    swap_recv,
    spread_send,
    spread_recv,
    back_send,
    back_recv,
    state_send,
    state_recv,
):
    tiles, steps, variables, cells, face_cells, modes, period = sizes
    share = steps // tiles
    tile = lax.axis_index("tile")
    plane = lax.axis_index("plane")
    inst = lax.axis_index("inst")
    other = 1 - plane
    mesh_id = pl.DeviceIdType.MESH
    others = [lax.rem(tile + j, tiles) for j in range(tiles)]

    own_copy = pltpu.make_async_copy(state, own, local_sem.at[0])
    own_copy.start()
    face_copy = pltpu.make_async_copy(boundary, faces, local_sem.at[1])
    face_copy.start()
    half_copy = pltpu.make_async_copy(boundary.at[:, plane], halves.at[plane], local_sem.at[2])
    half_copy.start()

    barrier = pltpu.get_barrier_semaphore()
    for j in range(tiles):
        if j:
            pl.semaphore_signal(
                barrier, inc=1, device_id={"tile": others[j]}, device_id_type=mesh_id
            )
        pl.semaphore_signal(
            barrier,
            inc=1,
            device_id={"tile": others[j], "plane": other},
            device_id_type=mesh_id,
        )
    pl.semaphore_signal(barrier, inc=1, device_id={"inst": 1 - inst}, device_id_type=mesh_id)
    pl.semaphore_wait(barrier, 2 * tiles)

    def remote(src, dst, send, recv, where):
        return pltpu.make_async_remote_copy(
            src_ref=src,
            dst_ref=dst,
            send_sem=send,
            recv_sem=recv,
            device_id=where,
            device_id_type=mesh_id,
        )

    def part(k):
        return pl.ds(k * share, share)

    swaps = []
    for j in [*range(1, tiles), 0]:
        swap = remote(
            boundary.at[part(others[j]), other],
            halves.at[plane, part(others[j])],
            swap_send.at[j],
            swap_recv.at[j],
            {"plane": other},
        )
        swap.start()
        swaps.append((j, swap))
    sent = []
    for j in range(1, tiles):
        copy = remote(
            boundary.at[part(others[j]), plane],
            spread.at[tile, plane],
            spread_send.at[j, 0],
            spread_recv.at[tile, plane],
            {"tile": others[j]},
        )
        copy.start()
        sent.append(copy)
    twin_copy = remote(state, twin, state_send.at[0], state_recv.at[0], {"inst": 1 - inst})
    twin_copy.start()
    home = pltpu.make_async_copy(
        boundary.at[part(tile), plane], spread.at[tile, plane], local_sem.at[3]
    )
    home.start()

    own_copy.wait()

    @pl.loop(0, steps)
    def _(t):
        for v in range(variables):
            edges[0, v, pl.ds(t, 1), :] = own[t, v, cells - 1 : cells, :]
            edges[1, v, pl.ds(t, 1), :] = own[t, v, 0:1, :]

    up = remote(
        edges.at[0], below, state_send.at[1], state_recv.at[1], {"tile": others[1]}
    )
    up.start()
    down = remote(
        edges.at[1], above, state_send.at[2], state_recv.at[2], {"tile": others[tiles - 1]}
    )
    down.start()

    for j, swap in swaps:
        swap.wait_recv()
        if j:
            copy = remote(
                halves.at[other, part(others[j])],
                spread.at[tile, other],
                spread_send.at[j, 1],
                spread_recv.at[tile, other],
                {"tile": others[j]},
            )
            copy.start()
            sent.append(copy)
    away = pltpu.make_async_copy(
        halves.at[other, part(tile)], spread.at[tile, other], local_sem.at[4]
    )
    away.start()
    beside_copy = remote(state, beside, state_send.at[3], state_recv.at[3], {"plane": other})
    beside_copy.start()

    count_row = jnp.where(plane == 0, counts[0:1, :], counts[1:2, :])
    stations = counts.shape[1]
    mode_row = lax.broadcasted_iota(jnp.int32, (period, stations), 0)
    mask = [
        (mode_row + a * period < count_row).astype(jnp.float32) for a in range(modes // period)
    ]
    resolved[...] = sum(mask[1:], mask[0])
    for k in range(gains.shape[0]):
        total = None
        for a in range(modes // period):
            column = columns[plane, a * period : (a + 1) * period, k : k + 1]
            term = mask[a] * jnp.broadcast_to(column, (period, stations))
            total = term if total is None else total + term
        gains[k] = total

    @pl.loop(0, 3 * steps)
    def _(e):
        taps_wide[e] = jnp.full((cells, stations), taps[e], jnp.float32)

    twin_copy.wait_recv()

    @pl.loop(0, variables)
    def _(v):
        @pl.loop(0, steps // 8)
        def _(block):
            base = steps - 8 * block
            held = {}

            def tap(offset):
                if offset not in held:
                    held[offset] = taps_wide[base + offset]
                return held[offset]

            sums = [None] * 8
            for source, shift in ((own, 0), (twin, steps)):
                for j in range(steps):
                    x = source[j, v]
                    for i in range(8):
                        term = tap(j - i + shift) * x
                        sums[i] = term if sums[i] is None else sums[i] + term
            for i in range(8):
                residual[8 * block + i, v] = sums[i]

    up.wait_recv()
    down.wait_recv()
    inv_volume = volume[0]
    row = lax.broadcasted_iota(jnp.int32, (cells, stations), 0)
    lane = lax.broadcasted_iota(jnp.int32, (cells, stations), 1)

    @pl.loop(0, steps)
    def _(t):
        around, across, rest = [], [], []
        for v in range(variables):
            s = own[t, v]
            ahead = jnp.where(
                row == cells - 1, above[v, pl.ds(t, 1), :], pltpu.roll(s, cells - 1, 0)
            )
            behind = jnp.where(row == 0, below[v, pl.ds(t, 1), :], pltpu.roll(s, 1, 0))
            outer = jnp.where(lane == stations - 1, 0.0, pltpu.roll(s, stations - 1, 1))
            inner = jnp.where(lane == 0, 0.0, pltpu.roll(s, 1, 1))
            around.append(0.5 * (ahead - behind))
            across.append(0.5 * (outer - inner))
            rest.append(DISSIPATION * (6.0 * s - (ahead + behind + outer + inner)))
        for u in range(variables):
            total = rest[u]
            for w in range(variables):
                total = total + flux_m[1, u, w] * around[w]
                total = total + flux_m[2, u, w] * across[w]
            residual[t, u] = residual[t, u] + inv_volume * total

    home.wait()
    away.wait()
    for j in range(1, tiles):
        for h in range(2):
            remote(
                spread.at[others[j], h],
                spread.at[others[j], h],
                spread_send.at[j, h],
                spread_recv.at[others[j], h],
                {"tile": others[j]},
            ).wait_recv()

    def correct(t):
        x = [
            jnp.concatenate(
                [spread[k, h, t, v] for k in range(tiles) for h in range(2)], axis=0
            )
            for v in range(variables)
        ]
        mixed = []
        for u in range(variables):
            total = left_m[u, 0] * x[0]
            for v in range(1, variables):
                total = total + left_m[u, v] * x[v]
            mixed.append(total)
        waves = jnp.dot(
            analysis[...],
            jnp.concatenate(mixed, axis=1),
            precision=precise,
            preferred_element_type=jnp.float32,
        )
        part_cos = [waves[:period, u * stations : (u + 1) * stations] for u in range(variables)]
        part_sin = [waves[period:, u * stations : (u + 1) * stations] for u in range(variables)]
        jumps = []
        outgoing = variables - NI
        for i in range(NI):
            jump_cos = -resolved[...] * part_cos[i]
            jump_sin = -resolved[...] * part_sin[i]
            for o in range(outgoing):
                real = gains[i * outgoing + o]
                imag = gains[(NI + i) * outgoing + o]
                jump_cos = jump_cos + real * part_cos[NI + o] - imag * part_sin[NI + o]
                jump_sin = jump_sin + imag * part_cos[NI + o] + real * part_sin[NI + o]
            jumps.append(jnp.concatenate([jump_cos, jump_sin], axis=0))
        delta = jnp.dot(
            synthesis[...],
            jnp.concatenate(jumps, axis=1),
            precision=precise,
            preferred_element_type=jnp.float32,
        )
        for k in range(tiles):
            for i in range(NI):
                block = delta[k * cells : (k + 1) * cells, i * stations : (i + 1) * stations]
                out8[k, t, i] = block
                out4[k, t, i] = jnp.where(plane == 0, block[face_cells:], block[:face_cells])

    @pl.loop(0, share // 2)
    def _(pair):
        correct(2 * pair)
        correct(2 * pair + 1)

    for j in range(1, tiles):
        copy = remote(
            out8.at[others[j]],
            in8.at[part(tile)],
            back_send.at[j, 0],
            back_recv.at[tile, 0],
            {"tile": others[j]},
        )
        copy.start()
        sent.append(copy)
    for j in [*range(1, tiles), 0]:
        copy = remote(
            out4.at[others[j]],
            in4.at[part(tile)],
            back_send.at[j, 1],
            back_recv.at[tile, 1],
            {"tile": others[j], "plane": other},
        )
        copy.start()
        sent.append(copy)
    keep = pltpu.make_async_copy(out8.at[tile], in8.at[part(tile)], local_sem.at[5])
    keep.start()

    half_copy.wait()
    beside_copy.wait_recv()
    sign = (1 - 2 * plane).astype(jnp.float32)
    axial_m = [
        [0.5 * sign * flux_m[0, u, w] for w in range(variables)] for u in range(variables)
    ]

    @pl.loop(0, steps)
    def _(t):
        slope, rest = [], []
        for v in range(variables):
            layer = beside[t, v]
            face = jnp.concatenate([halves[0, t, v], halves[1, t, v]], axis=0)
            slope.append(layer - face)
            rest.append(-DISSIPATION * (layer + face))
        for u in range(variables):
            total = rest[u]
            for w in range(variables):
                total = total + axial_m[u][w] * slope[w]
            residual[t, u] = residual[t, u] + inv_volume * total

    mixed_m = []
    for u in range(variables):
        line = []
        for i in range(NI):
            total = -DISSIPATION * right_m[u, i]
            for w in range(variables):
                total = total - axial_m[u][w] * right_m[w, i]
            line.append(total)
        mixed_m.append(line)

    face_copy.wait()
    keep.wait()
    for j in range(tiles):
        if j:
            remote(
                out8.at[others[j]],
                in8.at[part(others[j])],
                back_send.at[j, 0],
                back_recv.at[others[j], 0],
                {"tile": others[j]},
            ).wait_recv()
        remote(
            out4.at[others[j]],
            in4.at[part(others[j])],
            back_send.at[j, 1],
            back_recv.at[others[j], 1],
            {"tile": others[j], "plane": other},
        ).wait_recv()

    @pl.loop(0, steps)
    def _(t):
        near = [in8[t, i] for i in range(NI)]
        mine = [jnp.where(plane == 0, x[:face_cells], x[face_cells:]) for x in near]
        far = [in4[t, i] for i in range(NI)]
        for u in range(variables):
            total = mixed_m[u][0] * near[0]
            a = faces[t, plane, u] + right_m[u, 0] * mine[0]
            b = faces[t, other, u] + right_m[u, 0] * far[0]
            for i in range(1, NI):
                total = total + mixed_m[u][i] * near[i]
                a = a + right_m[u, i] * mine[i]
                b = b + right_m[u, i] * far[i]
            residual[t, u] = residual[t, u] + inv_volume * total
            corrected[t, plane, u] = a
            corrected[t, other, u] = b

    for _, swap in swaps:
        swap.wait_send()
    for copy in [*sent, twin_copy, up, down, beside_copy]:
        copy.wait_send()


def fast(
    state,
    boundary,
    inv_volume,
    flux_matrix,
    left_vectors,
    right_vectors,
    gain,
    harmonic_index,
    mode_count,
):
    tiles = lax.axis_size("tile")
    steps, variables, _, cells, stations = state.shape
    face_cells = boundary.shape[3]
    period = cells * tiles
    modes = gain.shape[2]
    share = steps // tiles
    columns = gain.transpose(0, 2, 1, 3, 4).reshape(gain.shape[0], modes, -1)
    offset = jnp.arange(3 * steps, dtype=jnp.int32) + steps
    product = offset[:, None] * harmonic_index[None, :] % (2 * steps)
    waves = jnp.sin(product.astype(jnp.float32) * (math.pi / steps))
    taps = jnp.sum(waves * harmonic_index.astype(jnp.float32)[None, :], axis=1) * (
        OMEGA_SCALE / steps
    )
    turns = np.outer(np.arange(period), np.arange(period)) % period * (2.0 * math.pi / period)
    analysis = np.concatenate([np.cos(turns), np.sin(turns)], axis=0) * (2.0 / period)
    synthesis = np.concatenate([np.cos(turns), np.sin(turns)], axis=1)
    vmem = pl.BlockSpec(memory_space=pltpu.VMEM)
    smem = pl.BlockSpec(memory_space=pltpu.SMEM)
    anywhere = pl.BlockSpec(memory_space=pl.ANY)
    sizes = (tiles, steps, variables, cells, face_cells, modes, period)
    f32 = jnp.float32
    dma = pltpu.SemaphoreType.DMA
    flat = (steps, variables, cells, stations)
    residual, corrected = pl.pallas_call(
        functools.partial(fast_kernel, sizes),
        out_shape=(
            jax.ShapeDtypeStruct(flat, f32),
            jax.ShapeDtypeStruct(boundary.shape, f32),
        ),
        in_specs=[anywhere, anywhere, vmem, smem, smem, smem, vmem, vmem, smem, vmem, vmem],
        out_specs=(vmem, vmem),
        scratch_shapes=[
            pltpu.VMEM(flat, f32),
            pltpu.VMEM(flat, f32),
            pltpu.VMEM(flat, f32),
            pltpu.VMEM(boundary.shape, f32),
            pltpu.VMEM((2, steps, variables, face_cells, stations), f32),
            pltpu.VMEM((tiles, 2, share, variables, face_cells, stations), f32),
            pltpu.VMEM((tiles, share, NI, cells, stations), f32),
            pltpu.VMEM((tiles, share, NI, face_cells, stations), f32),
            pltpu.VMEM((steps, NI, cells, stations), f32),
            pltpu.VMEM((steps, NI, face_cells, stations), f32),
            pltpu.VMEM((2, variables, steps, stations), f32),
            pltpu.VMEM((variables, steps, stations), f32),
            pltpu.VMEM((variables, steps, stations), f32),
            pltpu.VMEM((3 * steps, cells, stations), f32),
            pltpu.VMEM((columns.shape[2], period, stations), f32),
            pltpu.VMEM((period, stations), f32),
            dma((6,)),
            dma((tiles,)),
            dma((tiles,)),
            dma((tiles, 2)),
            dma((tiles, 2)),
            dma((tiles, 2)),
            dma((tiles, 2)),
            dma((4,)),
            dma((4,)),
        ],
        compiler_params=pltpu.CompilerParams(
            collective_id=0, has_side_effects=True, vmem_limit_bytes=32 * 1024 * 1024
        ),
        name="residual_kernel",
    )(
        state.reshape(flat),
        boundary,
        inv_volume,
        flux_matrix,
        left_vectors,
        right_vectors,
        columns,
        mode_count,
        taps,
        jnp.asarray(analysis, f32),
        jnp.asarray(synthesis, f32),
    )
    return (residual.reshape(state.shape), corrected)


def either(mesh):
    tiles, planes, insts = (mesh.shape[name] for name in ("tile", "plane", "inst"))

    def run(*args):
        state, boundary, gain = (args[0], args[1], args[6])
        steps, _, layers, cells, stations = state.shape
        modes, period = (gain.shape[2], cells * tiles)
        suits = (
            planes == boundary.shape[1] == 2
            and insts == 2
            and tiles > 2
            and steps % (2 * tiles) == 0
            and steps % 8 == 0
            and layers == 1
            and cells == 8
            and cells == 2 * boundary.shape[3]
            and stations % 128 == 0
            and modes % period == 0
        )
        return (fast if suits else local)(*args)

    return run


def solution(mesh):
    return jax.shard_map(
        either(mesh),
        mesh=mesh,
        in_specs=(
            P("inst", "groups", "plane", "tile", None),
            P("inst", None, "groups", ("tile", "plane"), None),
            P(("groups", "plane"), "tile", None),
            P("groups", None, None),
            P("groups", None),
            P("groups", None),
            P("groups", None, None, None, None),
            P("groups"),
            P("groups", None),
        ),
        out_specs=(
            P("inst", "groups", "plane", "tile", None),
            P("inst", None, "groups", ("tile", "plane"), None),
        ),
        check_vma=False,
    )
```

profile of v0, /device:TPU:0, one launch (start us, length us, event | category | flops | bytes accessed | tf_op | source)
XLA Modules:
  0.0 39.1 jit_solution(15153480722416794881)
XLA Ops:
  0.6 0.0 copy-start.9
  0.6 0.7 %convert_element_type.7 = f32[20]{0:T(128)S(1)} convert(s32[20]{0:T(128)} %param.18) | non-fusion elementwise | flops 20 | bytes 160 | tf_op jit(solution)/shard_map/convert_element_type | solution.py:550
  1.3 0.8 %fusion.4 = f32[72]{0:T(128)S(1)} fusion(f32[20]{0:T(128)S(1)} %convert_element_type.7, s32[20]{0:T(128)} %param.18, s32[72]{0:T(128)S(1)} %iota_add_fusion), kind=kLoop, calls=%fused_computation.5 | loop fusion | flops 15768 | bytes 736 | tf_op jit(solution)/shard_map/reduce_sum | solution.py:550
  2.1 0.0 copy-start.8
  2.1 0.0 copy-done.9
  2.2 0.7 %copy-done.8 = f32[2,2,64,2,3]{2,3,4,1,0:T(2,128)S(1)} copy-done((f32[2,2,64,2,3]{2,3,4,1,0:T(2,128)S(1)}, f32[2,2,64,2,3]{2,3,4,1,0:T(2,128)}, u32[]{:S(2)}) %copy-start.8) | copy-done | bytes 6168
  2.8 0.0 copy-start.2
  2.8 0.0 copy-start.3
  2.9 0.0 copy-start.4
  2.9 0.0 copy-start.5
  2.9 0.0 copy-start.6
  2.9 0.0 copy-start.7
  2.9 0.1 copy.22.columns
  3.0 0.6 %copy-done.2 = f32[64,32]{1,0:T(8,128)S(1)} copy-done((f32[64,32]{1,0:T(8,128)S(1)}, f32[64,32]{1,0:T(8,128)}, u32[]{:S(2)}) %copy-start.2) | copy-done | bytes 8216
  3.6 0.0 copy-done.3
  3.6 0.0 copy-done.4
  3.6 0.0 copy-done.5
  3.6 0.0 copy-done.6
  3.6 0.0 copy-done.7
  3.6 0.0 copy-start
  3.6 1.0 %copy-done = f32[24,5,1,8,128]{4,3,2,1,0:T(8,128)S(1)} copy-done((f32[24,5,1,8,128]{4,3,2,1,0:T(8,128)S(1)}, f32[24,5,1,8,128]{4,3,2,1,0:T(8,128)}, u32[]{:S(2)}) %copy-start) | copy-done | bytes 491544
  4.6 0.0 copy-start.1
  4.7 1.0 %copy-done.1 = f32[24,2,5,4,128]{4,3,2,1,0:T(4,128)S(1)} copy-done((f32[24,2,5,4,128]{4,3,2,1,0:T(4,128)S(1)}, f32[24,2,5,4,128]{4,3,2,1,0:T(4,128)}, u32[]{:S(2)}) %copy-start.1) | copy-done | bytes 491544
  5.7 31.9 %residual_kernel.1 = (f32[24,5,8,128]{3,2,1,0:T(8,128)S(1)}, f32[24,2,5,4,128]{4,3,2,1,0:T(4,128)S(1)}) custom-call(f32[24,5,8,128]{3,2,1,0:T(8,128)S(1)} %bitcast.6, f32[24,2,5,4,128]{4,3,2,1,0:T(4,128)S(1)} %copy-done.1, f32[1,8,128]{2,1,0:T(8,128)S(1)} %copy-done.4, f32[3,5,5]{2,1,0:T(8,128)S(1)} %copy.21.flux_m, f32[5,5]{1,0:T(8,128)S(1)} %copy-done.5, ...), custom_call_target="tpu_custom_call" | custom-call | tf_op jit(solution)/shard_map/residual_kernel/pallas_call | solution.py:563
  37.6 0.8 %copy.26 = f32[24,5,1,8,128]{4,3,2,1,0:T(8,128)} copy(f32[24,5,1,8,128]{4,3,2,1,0:T(8,128)S(1)} %bitcast.7) | data formatting | bytes 983040
  38.4 0.8 %copy.27 = f32[24,2,5,4,128]{4,3,2,1,0:T(4,128)} copy(f32[24,2,5,4,128]{4,3,2,1,0:T(4,128)S(1)} %get-tuple-element.15) | data formatting | bytes 983040
  (4 shorter events, 0.0 us)
Async XLA Ops:
  0.6 1.5 %copy-start.9 = (f32[3,5,5]{2,0,1:T(4,128)S(1)}, f32[3,5,5]{2,0,1:T(4,128)}, u32[]{:S(2)}) copy-start(f32[3,5,5]{2,0,1:T(4,128)} %param.14) | copy-start | bytes 904
  2.1 0.7 %copy-start.8 = (f32[2,2,64,2,3]{2,3,4,1,0:T(2,128)S(1)}, f32[2,2,64,2,3]{2,3,4,1,0:T(2,128)}, u32[]{:S(2)}) copy-start(f32[2,2,64,2,3]{2,3,4,1,0:T(2,128)} %param.17) | copy-start | bytes 18436
  2.8 0.8 %copy-start.2 = (f32[64,32]{1,0:T(8,128)S(1)}, f32[64,32]{1,0:T(8,128)}, u32[]{:S(2)}) copy-start(f32[64,32]{1,0:T(8,128)} %constant.24.clone.analysis) | copy-start | bytes 24580
  2.8 0.8 %copy-start.3 = (f32[32,64]{1,0:T(8,128)S(1)}, f32[32,64]{1,0:T(8,128)}, u32[]{:S(2)}) copy-start(f32[32,64]{1,0:T(8,128)} %constant.25.clone.synthesis) | copy-start | bytes 24580
  2.9 0.7 %copy-start.4 = (f32[1,8,128]{2,1,0:T(8,128)S(1)}, f32[1,8,128]{2,1,0:T(8,128)}, u32[]{:S(2)}) copy-start(f32[1,8,128]{2,1,0:T(8,128)} %volume.1) | copy-start | bytes 12292
  2.9 0.7 %copy-start.5 = (f32[5,5]{1,0:T(8,128)S(1)}, f32[5,5]{1,0:T(8,128)}, u32[]{:S(2)}) copy-start(f32[5,5]{1,0:T(8,128)} %left_m.1) | copy-start | bytes 304
  2.9 0.7 %copy-start.6 = (f32[5,5]{1,0:T(8,128)S(1)}, f32[5,5]{1,0:T(8,128)}, u32[]{:S(2)}) copy-start(f32[5,5]{1,0:T(8,128)} %right_m.1) | copy-start | bytes 304
  2.9 0.7 %copy-start.7 = (s32[2,128]{1,0:T(2,128)S(1)}, s32[2,128]{1,0:T(2,128)}, u32[]{:S(2)}) copy-start(s32[2,128]{1,0:T(2,128)} %counts.1) | copy-start | bytes 3076
  3.6 1.0 %copy-start = (f32[24,5,1,8,128]{4,3,2,1,0:T(8,128)S(1)}, f32[24,5,1,8,128]{4,3,2,1,0:T(8,128)}, u32[]{:S(2)}) copy-start(f32[24,5,1,8,128]{4,3,2,1,0:T(8,128)} %param.11) | copy-start | bytes 1474564
  4.6 1.0 %copy-start.1 = (f32[24,2,5,4,128]{4,3,2,1,0:T(4,128)S(1)}, f32[24,2,5,4,128]{4,3,2,1,0:T(4,128)}, u32[]{:S(2)}) copy-start(f32[24,2,5,4,128]{4,3,2,1,0:T(4,128)} %boundary.1) | copy-start | bytes 1474564
where the time goes:
time: 39.5 us; the launch traced here: 39.1 us
  Pallas kernels  31.9 us (81%)
  local copies, waits for them, and re-layouts  5.02 us (13%)
  other arithmetic  1.47 us (4%)
  between operations  0.75 us (2%)
    pallas_call x1, Pallas kernels, fast(): pl.pallas_call(functools.partial(fast_kernel, sizes), out_shape=(jax.Shap...  31.9 us
    unnamed x23, local copies, waits for them, and re-layouts  4.92 us
    reduce_sum x1, other arithmetic, fast(): jnp.sum(waves * harmonic_index.astype(jnp.float32)[None, :], axis=1)  0.8 us

commit v1 on v0

--- a/solution.py
+++ b/solution.py
@@ -159,7 +159,7 @@
     right_m,
     columns,
     counts,
-    taps,
+    harmonics,
     analysis,
     synthesis,
     residual,
@@ -171,7 +171,7 @@
     halves,
     spread,
     out8,
-    out4,
+    relay,
     in8,
     in4,
     edges,
@@ -192,6 +192,7 @@
 ):
     tiles, steps, variables, cells, face_cells, modes, period = sizes
     share = steps // tiles
+    piece = share // 2
     tile = lax.axis_index("tile")
     plane = lax.axis_index("plane")
     inst = lax.axis_index("inst")
@@ -207,19 +208,13 @@
     half_copy.start()
 
     barrier = pltpu.get_barrier_semaphore()
-    for j in range(tiles):
-        if j:
-            pl.semaphore_signal(
-                barrier, inc=1, device_id={"tile": others[j]}, device_id_type=mesh_id
-            )
+    for j in range(1, tiles):
         pl.semaphore_signal(
-            barrier,
-            inc=1,
-            device_id={"tile": others[j], "plane": other},
-            device_id_type=mesh_id,
-        )
+            barrier, inc=1, device_id={"tile": others[j]}, device_id_type=mesh_id
+        )
+    pl.semaphore_signal(barrier, inc=1, device_id={"plane": other}, device_id_type=mesh_id)
     pl.semaphore_signal(barrier, inc=1, device_id={"inst": 1 - inst}, device_id_type=mesh_id)
-    pl.semaphore_wait(barrier, 2 * tiles)
+    pl.semaphore_wait(barrier, tiles + 1)
 
     def remote(src, dst, send, recv, where):
         return pltpu.make_async_remote_copy(
@@ -231,35 +226,40 @@
             device_id_type=mesh_id,
         )
 
-    def part(k):
+    def part(k, h):
+        return pl.ds(k * share + h * piece, piece)
+
+    def whole(k):
         return pl.ds(k * share, share)
 
+    order = [(j, h) for h in range(2) for j in [*range(1, tiles), 0]]
     swaps = []
-    for j in [*range(1, tiles), 0]:
+    for j, h in order:
         swap = remote(
-            boundary.at[part(others[j]), other],
-            halves.at[plane, part(others[j])],
-            swap_send.at[j],
-            swap_recv.at[j],
+            boundary.at[part(others[j], h), other],
+            halves.at[plane, part(others[j], h)],
+            swap_send.at[j, h],
+            swap_recv.at[j, h],
             {"plane": other},
         )
         swap.start()
-        swaps.append((j, swap))
+        swaps.append((j, h, swap))
     sent = []
-    for j in range(1, tiles):
-        copy = remote(
-            boundary.at[part(others[j]), plane],
-            spread.at[tile, plane],
-            spread_send.at[j, 0],
-            spread_recv.at[tile, plane],
-            {"tile": others[j]},
-        )
-        copy.start()
-        sent.append(copy)
+    for j, h in order:
+        if j:
+            copy = remote(
+                boundary.at[part(others[j], h), plane],
+                spread.at[tile, plane, h * piece : (h + 1) * piece],
+                spread_send.at[j, 0, h],
+                spread_recv.at[tile, plane, h],
+                {"tile": others[j]},
+            )
+            copy.start()
+            sent.append(copy)
     twin_copy = remote(state, twin, state_send.at[0], state_recv.at[0], {"inst": 1 - inst})
     twin_copy.start()
     home = pltpu.make_async_copy(
-        boundary.at[part(tile), plane], spread.at[tile, plane], local_sem.at[3]
+        boundary.at[whole(tile), plane], spread.at[tile, plane], local_sem.at[3]
     )
     home.start()
 
@@ -280,24 +280,25 @@
     )
     down.start()
 
-    for j, swap in swaps:
+    beside_copy = remote(state, beside, state_send.at[3], state_recv.at[3], {"plane": other})
+    for place, (j, h, swap) in enumerate(swaps):
+        if place == len(swaps) - 1:
+            beside_copy.start()
         swap.wait_recv()
         if j:
             copy = remote(
-                halves.at[other, part(others[j])],
-                spread.at[tile, other],
-                spread_send.at[j, 1],
-                spread_recv.at[tile, other],
+                halves.at[other, part(others[j], h)],
+                spread.at[tile, other, h * piece : (h + 1) * piece],
+                spread_send.at[j, 1, h],
+                spread_recv.at[tile, other, h],
                 {"tile": others[j]},
             )
             copy.start()
             sent.append(copy)
     away = pltpu.make_async_copy(
-        halves.at[other, part(tile)], spread.at[tile, other], local_sem.at[4]
+        halves.at[other, whole(tile)], spread.at[tile, other], local_sem.at[4]
     )
     away.start()
-    beside_copy = remote(state, beside, state_send.at[3], state_recv.at[3], {"plane": other})
-    beside_copy.start()
 
     count_row = jnp.where(plane == 0, counts[0:1, :], counts[1:2, :])
     stations = counts.shape[1]
@@ -314,9 +315,27 @@
             total = term if total is None else total + term
         gains[k] = total
 
-    @pl.loop(0, 3 * steps)
-    def _(e):
-        taps_wide[e] = jnp.full((cells, stations), taps[e], jnp.float32)
+    number = harmonics.shape[0]
+    padded = -(-number // 8) * 8
+    depth = lax.broadcasted_iota(jnp.int32, (padded, stations), 0)
+    distance = lax.broadcasted_iota(jnp.int32, (padded, stations), 1).astype(jnp.float32) + steps
+    frequency = jnp.zeros((padded, stations), jnp.float32)
+    for k in range(number):
+        frequency = jnp.where(depth == k, harmonics[k].astype(jnp.float32), frequency)
+    turn = frequency * distance
+    turn = turn - 2.0 * steps * jnp.floor((turn + 0.5) * (0.5 / steps))
+    turn = jnp.where(turn > steps, turn - 2.0 * steps, turn)
+    turn = jnp.where(turn > 0.5 * steps, steps - turn, turn)
+    turn = jnp.where(turn < -0.5 * steps, -steps - turn, turn)
+    angle = turn * (math.pi / steps)
+    square = angle * angle
+    series = jnp.full((padded, stations), -1.0 / math.factorial(15), jnp.float32)
+    for n in range(13, 0, -2):
+        series = series * square + (1.0 if n % 4 == 1 else -1.0) / math.factorial(n)
+    weights = jnp.sum(frequency * angle * series, axis=0, keepdims=True) * (OMEGA_SCALE / steps)
+    weights = jnp.broadcast_to(weights, (cells, stations))
+    for e in range(3 * steps):
+        taps_wide[e] = jnp.broadcast_to(weights[:, e : e + 1], (cells, stations))
 
     twin_copy.wait_recv()
 
@@ -369,18 +388,6 @@
                 total = total + flux_m[2, u, w] * across[w]
             residual[t, u] = residual[t, u] + inv_volume * total
 
-    home.wait()
-    away.wait()
-    for j in range(1, tiles):
-        for h in range(2):
-            remote(
-                spread.at[others[j], h],
-                spread.at[others[j], h],
-                spread_send.at[j, h],
-                spread_recv.at[others[j], h],
-                {"tile": others[j]},
-            ).wait_recv()
-
     def correct(t):
         x = [
             jnp.concatenate(
@@ -423,37 +430,72 @@
             for i in range(NI):
                 block = delta[k * cells : (k + 1) * cells, i * stations : (i + 1) * stations]
                 out8[k, t, i] = block
-                out4[k, t, i] = jnp.where(plane == 0, block[face_cells:], block[:face_cells])
-
-    @pl.loop(0, share // 2)
-    def _(pair):
-        correct(2 * pair)
-        correct(2 * pair + 1)
-
-    for j in range(1, tiles):
-        copy = remote(
-            out8.at[others[j]],
-            in8.at[part(tile)],
-            back_send.at[j, 0],
-            back_recv.at[tile, 0],
-            {"tile": others[j]},
-        )
-        copy.start()
-        sent.append(copy)
-    for j in [*range(1, tiles), 0]:
-        copy = remote(
-            out4.at[others[j]],
-            in4.at[part(tile)],
-            back_send.at[j, 1],
-            back_recv.at[tile, 1],
-            {"tile": others[j], "plane": other},
-        )
-        copy.start()
-        sent.append(copy)
-    keep = pltpu.make_async_copy(out8.at[tile], in8.at[part(tile)], local_sem.at[5])
-    keep.start()
+
+    home.wait()
+    away.wait()
+    keeps = []
+    for h in range(2):
+        for j in range(1, tiles):
+            for side in range(2):
+                span = spread.at[others[j], side, h * piece : (h + 1) * piece]
+                remote(
+                    span,
+                    span,
+                    spread_send.at[j, side, h],
+                    spread_recv.at[others[j], side, h],
+                    {"tile": others[j]},
+                ).wait_recv()
+        for t in range(piece):
+            correct(h * piece + t)
+        for j in range(1, tiles):
+            copy = remote(
+                out8.at[others[j], h * piece : (h + 1) * piece],
+                in8.at[part(tile, h)],
+                back_send.at[j, 0, h],
+                back_recv.at[tile, 0, h],
+                {"tile": others[j]},
+            )
+            copy.start()
+            sent.append(copy)
+        keep = pltpu.make_async_copy(
+            out8.at[tile, h * piece : (h + 1) * piece],
+            in8.at[part(tile, h)],
+            local_sem.at[5 + h],
+        )
+        keep.start()
+        keeps.append(keep)
 
     half_copy.wait()
+    for h in range(2):
+        for j in range(tiles):
+            source = others[j]
+            if j:
+                remote(
+                    out8.at[source, h * piece : (h + 1) * piece],
+                    in8.at[part(source, h)],
+                    back_send.at[j, 0, h],
+                    back_recv.at[source, 0, h],
+                    {"tile": source},
+                ).wait_recv()
+            else:
+                keeps[h].wait()
+            first = source * share + h * piece
+            for t in range(piece):
+                for i in range(NI):
+                    block = in8[first + t, i]
+                    relay[first + t, i] = jnp.where(
+                        plane == 0, block[face_cells:], block[:face_cells]
+                    )
+            copy = remote(
+                relay.at[part(source, h)],
+                in4.at[part(source, h)],
+                back_send.at[j, 1, h],
+                back_recv.at[j, 1, h],
+                {"plane": other},
+            )
+            copy.start()
+            sent.append(copy)
+
     beside_copy.wait_recv()
     sign = (1 - 2 * plane).astype(jnp.float32)
     axial_m = [
@@ -485,23 +527,15 @@
         mixed_m.append(line)
 
     face_copy.wait()
-    keep.wait()
-    for j in range(tiles):
-        if j:
+    for h in range(2):
+        for j in range(tiles):
             remote(
-                out8.at[others[j]],
-                in8.at[part(others[j])],
-                back_send.at[j, 0],
-                back_recv.at[others[j], 0],
-                {"tile": others[j]},
+                relay.at[part(others[j], h)],
+                in4.at[part(others[j], h)],
+                back_send.at[j, 1, h],
+                back_recv.at[j, 1, h],
+                {"plane": other},
             ).wait_recv()
-        remote(
-            out4.at[others[j]],
-            in4.at[part(others[j])],
-            back_send.at[j, 1],
-            back_recv.at[others[j], 1],
-            {"tile": others[j], "plane": other},
-        ).wait_recv()
 
     @pl.loop(0, steps)
     def _(t):
@@ -520,7 +554,7 @@
             corrected[t, plane, u] = a
             corrected[t, other, u] = b
 
-    for _, swap in swaps:
+    for _, _, swap in swaps:
         swap.wait_send()
     for copy in [*sent, twin_copy, up, down, beside_copy]:
         copy.wait_send()
@@ -544,12 +578,6 @@
     modes = gain.shape[2]
     share = steps // tiles
     columns = gain.transpose(0, 2, 1, 3, 4).reshape(gain.shape[0], modes, -1)
-    offset = jnp.arange(3 * steps, dtype=jnp.int32) + steps
-    product = offset[:, None] * harmonic_index[None, :] % (2 * steps)
-    waves = jnp.sin(product.astype(jnp.float32) * (math.pi / steps))
-    taps = jnp.sum(waves * harmonic_index.astype(jnp.float32)[None, :], axis=1) * (
-        OMEGA_SCALE / steps
-    )
     turns = np.outer(np.arange(period), np.arange(period)) % period * (2.0 * math.pi / period)
     analysis = np.concatenate([np.cos(turns), np.sin(turns)], axis=0) * (2.0 / period)
     synthesis = np.concatenate([np.cos(turns), np.sin(turns)], axis=1)
@@ -576,7 +604,7 @@
             pltpu.VMEM((2, steps, variables, face_cells, stations), f32),
             pltpu.VMEM((tiles, 2, share, variables, face_cells, stations), f32),
             pltpu.VMEM((tiles, share, NI, cells, stations), f32),
-            pltpu.VMEM((tiles, share, NI, face_cells, stations), f32),
+            pltpu.VMEM((steps, NI, face_cells, stations), f32),
             pltpu.VMEM((steps, NI, cells, stations), f32),
             pltpu.VMEM((steps, NI, face_cells, stations), f32),
             pltpu.VMEM((2, variables, steps, stations), f32),
@@ -585,13 +613,13 @@
             pltpu.VMEM((3 * steps, cells, stations), f32),
             pltpu.VMEM((columns.shape[2], period, stations), f32),
             pltpu.VMEM((period, stations), f32),
-            dma((6,)),
-            dma((tiles,)),
-            dma((tiles,)),
+            dma((7,)),
             dma((tiles, 2)),
             dma((tiles, 2)),
-            dma((tiles, 2)),
-            dma((tiles, 2)),
+            dma((tiles, 2, 2)),
+            dma((tiles, 2, 2)),
+            dma((tiles, 2, 2)),
+            dma((tiles, 2, 2)),
             dma((4,)),
             dma((4,)),
         ],
@@ -608,7 +636,7 @@
         right_vectors,
         columns,
         mode_count,
-        taps,
+        harmonic_index,
         jnp.asarray(analysis, f32),
         jnp.asarray(synthesis, f32),
     )
@@ -632,6 +660,7 @@
             and cells == 8
             and cells == 2 * boundary.shape[3]
             and stations % 128 == 0
+            and 3 * steps <= stations
             and modes % period == 0
         )
         return (fast if suits else local)(*args)

time: 39.5 us -> 37.9 us (0.959)
  other arithmetic: 1.47 us -> 0 us
    reduce_sum x1 -> x0, other arithmetic: 0.8 us -> none  [fast(): jnp.sum(waves * harmonic_index.astype(jnp.float32)[None, :], axis=1)]
    convert_element_type x1 -> x0, other arithmetic: 0.66 us -> none  [fast(): harmonic_index.astype(jnp.float32)[None, :]]
where the time goes in v1:
time: 37.9 us; the launch traced here: 37.5 us
  Pallas kernels  31.8 us (84%)
  local copies, waits for them, and re-layouts  5.05 us (13%)
  between operations  0.74 us (2%)
    pallas_call x1, Pallas kernels, fast(): pl.pallas_call(functools.partial(fast_kernel, sizes), out_shape=(jax.Shap...  31.8 us
    unnamed x23, local copies, waits for them, and re-layouts  4.95 us

profile of v1, /device:TPU:0, one launch (start us, length us, event | category | flops | bytes accessed | tf_op | source)
XLA Modules:
  0.0 37.5 jit_solution(17426143362300189472)
XLA Ops:
  0.6 0.0 copy-start.9
  0.6 0.7 %copy.17.flux_m = f32[3,5,5]{2,1,0:T(8,128)S(1)} copy(f32[3,5,5]{2,0,1:T(4,128)} %param.14) | data formatting | bytes 600 | tf_op args[3]
  1.4 0.0 copy-done.9
  1.4 0.0 copy-start.2
  1.4 0.0 copy-start.3
  1.4 0.0 copy-start.4
  1.4 0.0 copy-start.5
  1.4 0.0 copy-start.6
  1.4 0.0 copy-start.7
  1.4 0.0 copy-start.8
  1.4 0.1 copy.18.columns
  1.5 0.6 %copy-done.2 = f32[64,32]{1,0:T(8,128)S(1)} copy-done((f32[64,32]{1,0:T(8,128)S(1)}, f32[64,32]{1,0:T(8,128)}, u32[]{:S(2)}) %copy-start.2) | copy-done | bytes 8216
  2.1 0.0 copy-done.3
  2.1 0.0 copy-done.4
  2.1 0.0 copy-done.5
  2.1 0.0 copy-done.6
  2.1 0.0 copy-done.7
  2.1 0.0 copy-done.8
  2.2 0.0 copy-start
  2.2 1.0 %copy-done = f32[24,5,1,8,128]{4,3,2,1,0:T(8,128)S(1)} copy-done((f32[24,5,1,8,128]{4,3,2,1,0:T(8,128)S(1)}, f32[24,5,1,8,128]{4,3,2,1,0:T(8,128)}, u32[]{:S(2)}) %copy-start) | copy-done | bytes 491544
  3.2 0.0 copy-start.1
  3.2 1.0 %copy-done.1 = f32[24,2,5,4,128]{4,3,2,1,0:T(4,128)S(1)} copy-done((f32[24,2,5,4,128]{4,3,2,1,0:T(4,128)S(1)}, f32[24,2,5,4,128]{4,3,2,1,0:T(4,128)}, u32[]{:S(2)}) %copy-start.1) | copy-done | bytes 491544
  4.2 31.8 %residual_kernel.1 = (f32[24,5,8,128]{3,2,1,0:T(8,128)S(1)}, f32[24,2,5,4,128]{4,3,2,1,0:T(4,128)S(1)}) custom-call(f32[24,5,8,128]{3,2,1,0:T(8,128)S(1)} %bitcast.6, f32[24,2,5,4,128]{4,3,2,1,0:T(4,128)S(1)} %copy-done.1, f32[1,8,128]{2,1,0:T(8,128)S(1)} %copy-done.4, f32[3,5,5]{2,1,0:T(8,128)S(1)} %copy.17.flux_m, f32[5,5]{1,0:T(8,128)S(1)} %copy-done.5, ...), custom_call_target="tpu_custom_call" | custom-call | tf_op jit(solution)/shard_map/residual_kernel/pallas_call | solution.py:591
  36.0 0.8 %copy.22 = f32[24,5,1,8,128]{4,3,2,1,0:T(8,128)} copy(f32[24,5,1,8,128]{4,3,2,1,0:T(8,128)S(1)} %bitcast.7) | data formatting | bytes 983040
  36.8 0.8 %copy.23 = f32[24,2,5,4,128]{4,3,2,1,0:T(4,128)} copy(f32[24,2,5,4,128]{4,3,2,1,0:T(4,128)S(1)} %get-tuple-element.13) | data formatting | bytes 983040
  (1 shorter events, 0.0 us)
Async XLA Ops:
  0.6 0.7 %copy-start.9 = (f32[2,2,64,2,3]{2,3,4,1,0:T(2,128)S(1)}, f32[2,2,64,2,3]{2,3,4,1,0:T(2,128)}, u32[]{:S(2)}) copy-start(f32[2,2,64,2,3]{2,3,4,1,0:T(2,128)} %param.17) | copy-start | bytes 18436
  1.4 0.8 %copy-start.2 = (f32[64,32]{1,0:T(8,128)S(1)}, f32[64,32]{1,0:T(8,128)}, u32[]{:S(2)}) copy-start(f32[64,32]{1,0:T(8,128)} %constant.4.clone.analysis) | copy-start | bytes 24580
  1.4 0.8 %copy-start.3 = (f32[32,64]{1,0:T(8,128)S(1)}, f32[32,64]{1,0:T(8,128)}, u32[]{:S(2)}) copy-start(f32[32,64]{1,0:T(8,128)} %constant.5.clone.synthesis) | copy-start | bytes 24580
  1.4 0.7 %copy-start.4 = (f32[1,8,128]{2,1,0:T(8,128)S(1)}, f32[1,8,128]{2,1,0:T(8,128)}, u32[]{:S(2)}) copy-start(f32[1,8,128]{2,1,0:T(8,128)} %volume.1) | copy-start | bytes 12292
  1.4 0.7 %copy-start.5 = (f32[5,5]{1,0:T(8,128)S(1)}, f32[5,5]{1,0:T(8,128)}, u32[]{:S(2)}) copy-start(f32[5,5]{1,0:T(8,128)} %left_m.1) | copy-start | bytes 304
  1.4 0.7 %copy-start.6 = (f32[5,5]{1,0:T(8,128)S(1)}, f32[5,5]{1,0:T(8,128)}, u32[]{:S(2)}) copy-start(f32[5,5]{1,0:T(8,128)} %right_m.1) | copy-start | bytes 304
  1.4 0.7 %copy-start.7 = (s32[2,128]{1,0:T(2,128)S(1)}, s32[2,128]{1,0:T(2,128)}, u32[]{:S(2)}) copy-start(s32[2,128]{1,0:T(2,128)} %counts.1) | copy-start | bytes 3076
  1.4 0.7 %copy-start.8 = (s32[20]{0:T(128)S(1)}, s32[20]{0:T(128)}, u32[]{:S(2)}) copy-start(s32[20]{0:T(128)} %harmonics.1) | copy-start | bytes 244
  2.2 1.0 %copy-start = (f32[24,5,1,8,128]{4,3,2,1,0:T(8,128)S(1)}, f32[24,5,1,8,128]{4,3,2,1,0:T(8,128)}, u32[]{:S(2)}) copy-start(f32[24,5,1,8,128]{4,3,2,1,0:T(8,128)} %param.11) | copy-start | bytes 1474564
  3.2 1.0 %copy-start.1 = (f32[24,2,5,4,128]{4,3,2,1,0:T(4,128)S(1)}, f32[24,2,5,4,128]{4,3,2,1,0:T(4,128)}, u32[]{:S(2)}) copy-start(f32[24,2,5,4,128]{4,3,2,1,0:T(4,128)} %boundary.1) | copy-start | bytes 1474564
